TPU v7x, 256 devices: a whole 4x4x8 slice. The times are simulated.
256 devices in a mesh: row: 8 (over z), col: 32 (over y, x, core).
Axes of the slice: x: 4, y: 4, z: 8, core: 2. Of those that a mesh axis runs over, the one named last changes fastest.
Arguments:
- tokens: bfloat16 [2560, 5120], P('col', 'row'), may hold values from -6 to 6
- cotangent: bfloat16 [2560, 5120], P('col', 'row'), may hold values from -1.5 to 1.5
- gate_weight: bfloat16 [5120, 8192], P('row', 'col'), may hold values from -0.078125 to 0.078125
- up_weight: bfloat16 [5120, 8192], P('row', 'col'), may hold values from -0.078125 to 0.078125
- down_weight: bfloat16 [8192, 5120], P('col', 'row'), may hold values from -0.0625 to 0.0625
Outputs:
- grad_tokens: float32 [2560, 5120], P('col', 'row')
- grad_gate_weight: float32 [5120, 8192], P('row', 'col')
- grad_up_weight: float32 [5120, 8192], P('row', 'col')
- grad_down_weight: float32 [8192, 5120], P('col', 'row')
All inputs are finite; a program needn't handle non-finite values.
Results may differ from a plain program's by a relative error of at most 0.0029.
Values may be sent and summed in bfloat16 or wider, within the bound.
A program may use at most 64 MiB of HBM per device.

v0:
```python
import jax
import jax.numpy as jnp
from jax import lax
from jax.sharding import PartitionSpec as P


def swiglu_backward(gate_proj, up_proj, grad_hidden):
    sigmoid_gate = jax.nn.sigmoid(gate_proj)
    silu_gate = gate_proj * sigmoid_gate
    hidden = (silu_gate * up_proj).astype(jnp.bfloat16)
    grad_up = (grad_hidden * silu_gate).astype(jnp.bfloat16)
    grad_gate = (
        grad_hidden * up_proj * sigmoid_gate * (1.0 + gate_proj * (1.0 - sigmoid_gate))
    ).astype(jnp.bfloat16)
    return (hidden, grad_gate, grad_up)


def per_device(tokens, cotangent, gate_weight, up_weight, down_weight):
    contract_rows = (((0,), (0,)), ((), ()))
    contract_cols = (((1,), (1,)), ((), ()))
    tok_rows = lax.all_gather(tokens, "col", axis=0, tiled=True)
    gate_proj = jnp.dot(tok_rows, gate_weight, preferred_element_type=jnp.float32)
    up_proj = jnp.dot(tok_rows, up_weight, preferred_element_type=jnp.float32)
    cot_rows = lax.all_gather(cotangent, "col", axis=0, tiled=True)
    hidden_part = lax.dot_general(
        cot_rows, down_weight, contract_cols, preferred_element_type=jnp.float32
    )
    gate_proj, up_proj = lax.psum((gate_proj, up_proj), "row")
    grad_hidden = lax.psum(hidden_part, "row")
    hidden, grad_gate, grad_up = swiglu_backward(gate_proj, up_proj, grad_hidden)
    grad_down_weight = lax.dot_general(
        hidden, cot_rows, contract_rows, preferred_element_type=jnp.float32
    )
    grad_gate_weight = lax.dot_general(
        tok_rows, grad_gate, contract_rows, preferred_element_type=jnp.float32
    )
    grad_up_weight = lax.dot_general(
        tok_rows, grad_up, contract_rows, preferred_element_type=jnp.float32
    )
    result = lax.dot_general(
        grad_gate, gate_weight, contract_cols, preferred_element_type=jnp.float32
    )
    grad_tokens = lax.psum_scatter(
        result
        + lax.dot_general(grad_up, up_weight, contract_cols, preferred_element_type=jnp.float32),
        "col",
        scatter_dimension=0,
        tiled=True,
    )
    return (grad_tokens, grad_gate_weight, grad_up_weight, grad_down_weight)


def solution(mesh):
    in_specs = (P("col", "row"), P("col", "row"), P("row", "col"), P("row", "col"), P("col", "row"))
    out_specs = (P("col", "row"), P("row", "col"), P("row", "col"), P("col", "row"))
    return jax.shard_map(
        per_device, mesh=mesh, in_specs=in_specs, out_specs=out_specs, check_vma=False
    )
```

profile of v0, /device:TPU:1, one launch (start us, length us, event | category | flops | bytes accessed | tf_op | source)
XLA Modules:
  0.0 408.3 jit_solution(4371109135493497093)
XLA Ops:
  7.2 0.0 copy-start
  7.2 0.0 all-gather.5.cloned.1.call-start
  7.2 0.7 all-gather.5.cloned.1.call-update
  7.9 0.0 all-gather.3.cloned.1.call-start
  8.0 0.7 all-gather.3.cloned.1.call-update
  8.7 0.0 copy-start.2
  8.7 0.0 all-reduce.3.cloned.1.call-start
  8.7 56.5 %all-gather.5.cloned.1.call-done = bf16[2560,640]{1,0:T(8,128)(2,1)} async-done(((bf16[80,640]{1,0:T(8,128)(2,1)}), bf16[2560,640]{1,0:T(8,128)(2,1)}) %all-gather.5.cloned.1.call-update) | async-done | bytes 3276816 | tf_op jit(solution)/shard_map/all_gather | solution.py:21
  65.2 0.0 copy-done
  65.2 0.0 copy-start.1
  65.2 4.7 %fusion.6 = f32[2560,256]{1,0:T(8,128)} fusion(bf16[2560,640]{1,0:T(8,128)(2,1)} %all-gather.5.cloned.1.call-done, bf16[640,256]{1,0:T(8,128)(2,1)S(1)} %copy-done), kind=kOutput, calls=%fused_computation.12 | convolution fusion | flops 838860800 | bytes 6225920 | tf_op jit(solution)/shard_map/dot_general | solution.py:22
  70.0 0.0 copy-done.2
  70.0 0.0 copy-done.1
  70.0 0.0 copy-start.3
  70.0 2.8 fusion.5
  72.8 44.9 %all-gather.3.cloned.1.call-done = bf16[2560,640]{1,0:T(8,128)(2,1)} async-done(((bf16[80,640]{1,0:T(8,128)(2,1)}), bf16[2560,640]{1,0:T(8,128)(2,1)}) %all-gather.3.cloned.1.call-update) | async-done | bytes 3276816 | tf_op jit(solution)/shard_map/all_gather | solution.py:24
  117.7 0.0 copy-done.3
  117.7 4.7 %fusion.4 = f32[2560,256]{1,0:T(8,128)} fusion(bf16[2560,640]{1,0:T(8,128)(2,1)} %all-gather.3.cloned.1.call-done, bf16[256,640]{1,0:T(8,128)(2,1)S(1)} %copy-done.3), kind=kOutput, calls=%fused_computation.10 | convolution fusion | flops 838860800 | bytes 6225920 | tf_op jit(solution)/shard_map/dot_general | solution.py:25
  122.4 0.0 all-reduce.3.cloned.1.call-update
  122.4 0.0 reduce-scatter.2.cloned.1.call-start
  122.4 178.1 %all-reduce.3.cloned.1.call-done = (f32[2560,256]{1,0:T(8,128)}, f32[2560,256]{1,0:T(8,128)}, f32[2560,256]{1,0:T(8,128)}) async-done(((f32[2560,256]{1,0:T(8,128)}, f32[2560,256]{1,0:T(8,128)}, f32[2560,256]{1,0:T(8,128)}), (f32[2560,256]{1,0:T(8,128)}, f32[2560,256]{1,0:T(8,128)}, f32[2560,256]{1,0:T(8,128)})) %all-reduce.3.cloned.1.call-update) | async-done | bytes 7864336 | tf_op jit(solution)/shard_map/psum | solution.py:28
  300.5 4.5 %multiply_convert_fusion.1 = (bf16[2560,256]{1,0:T(8,128)(2,1)S(1)}, bf16[2560,256]{1,0:T(8,128)(2,1)S(1)}) fusion(f32[2560,256]{1,0:T(8,128)} %get-tuple-element.9, f32[2560,256]{1,0:T(8,128)} %get-tuple-element.8, f32[2560,256]{1,0:T(8,128)} %get-tuple-element.10), kind=kLoop, calls=%fused_computation.2 | loop fusion | flops 8519680 | bytes 10485760 | tf_op jit(solution)/shard_map/convert_element_type | solution.py:11
  305.0 1.2 fusion.7
  306.2 4.0 convolution_add_fusion
  310.2 0.0 reduce-scatter.2.cloned.1.call-update
  310.2 4.0 convolution_bitcast_fusion.1
  314.2 2.2 copy.9
  316.3 3.1 convolution_bitcast_fusion
  319.5 1.1 copy.10
  320.5 5.9 %fusion.1 = f32[256,640]{1,0:T(8,128)} fusion(bf16[2560,640]{1,0:T(8,128)(2,1)} %all-gather.3.cloned.1.call-done, f32[2560,256]{1,0:T(8,128)} %get-tuple-element.10, f32[2560,256]{1,0:T(8,128)} %get-tuple-element.8), kind=kOutput, calls=%fused_computation.6 | convolution fusion | flops 842792960 | bytes 9175040 | tf_op jit(solution)/shard_map/dot_general | solution.py:31
  326.4 75.3 %reduce-scatter.2.cloned.1.call-done = f32[80,640]{1,0:T(8,128)} async-done(((f32[2560,640]{1,0:T(8,128)}), f32[80,640]{1,0:T(8,128)}) %reduce-scatter.2.cloned.1.call-update) | async-done | bytes 204816 | tf_op jit(solution)/shard_map/reduce_scatter | solution.py:43
Async XLA Ops:
  7.2 58.1 %copy-start = (bf16[640,256]{1,0:T(8,128)(2,1)S(1)}, bf16[640,256]{1,0:T(8,128)(2,1)}, u32[]{:S(2)}) copy-start(bf16[640,256]{1,0:T(8,128)(2,1)} %param.7) | copy-start | bytes 983044
  7.2 58.0 %all-gather.5.cloned.1.call-start = ((), (), s32[]{:S(2)}) async-start(), calls=%async_computation.2 | async-start | bytes 3379200 | tf_op jit(solution)/shard_map/all_gather | solution.py:21
  7.9 109.8 %all-gather.3.cloned.1.call-start = ((), (), s32[]{:S(2)}) async-start(), calls=%async_computation.1 | async-start | bytes 3379200 | tf_op jit(solution)/shard_map/all_gather | solution.py:24
  8.7 61.3 %copy-start.2 = (bf16[640,256]{1,0:T(8,128)(2,1)S(1)}, bf16[640,256]{1,0:T(8,128)(2,1)}, u32[]{:S(2)}) copy-start(bf16[640,256]{1,0:T(8,128)(2,1)} %param.8) | copy-start | bytes 983044
  8.7 291.8 %all-reduce.3.cloned.1.call-start = ((), (), s32[]{:S(2)}) async-start(), calls=%async_computation.4 | async-start | bytes 15728640 | tf_op jit(solution)/shard_map/psum | solution.py:28
  65.2 4.7 %copy-start.1 = (bf16[2560,640]{1,0:T(8,128)(2,1)S(1)}, bf16[2560,640]{1,0:T(8,128)(2,1)}, u32[]{:S(2)}) copy-start(bf16[2560,640]{1,0:T(8,128)(2,1)} %all-gather.5.cloned.1.call-done) | copy-start | bytes 9830404
  70.0 47.7 %copy-start.3 = (bf16[256,640]{1,0:T(8,128)(2,1)S(1)}, bf16[256,640]{1,0:T(8,128)(2,1)}, u32[]{:S(2)}) copy-start(bf16[256,640]{1,0:T(8,128)(2,1)} %param.9) | copy-start | bytes 983044
  122.4 279.4 %reduce-scatter.2.cloned.1.call-start = ((), (), s32[]{:S(2)}) async-start(), calls=%async_computation.3 | async-start | bytes 6758400 | tf_op jit(solution)/shard_map/reduce_scatter | solution.py:43
Sparse Core Ops, SparseCore 0:
  10.6 54.5 all-gather.4
  67.8 49.8 all-gather.2
  122.5 177.9 all-reduce.2
  310.3 91.3 reduce-scatter.1
where the time goes:
time: 409 us; the launch traced here: 408 us
  waiting for transfers between devices  356 us (87%)
  matrix products  30.4 us (7%)
  between operations  13.8 us (3%)
  other arithmetic  4.5 us (1%)
    psum x1, waiting for transfers between devices, per_device(): gate_proj, up_proj = lax.psum((gate_proj, up_proj), 'row')  178 us
    reduce_scatter x1, waiting for transfers between devices, per_device(): lax.psum_scatter(result + lax.dot_general(grad_up, up_weight, contract_co...  75.3 us
    all_gather x1, waiting for transfers between devices, per_device(): tok_rows = lax.all_gather(tokens, 'col', axis=0, tiled=True)  56.5 us
    all_gather x1, waiting for transfers between devices, per_device(): cot_rows = lax.all_gather(cotangent, 'col', axis=0, tiled=True)  44.9 us
  transfers between devices with their start and end apart: 4, of which 4 were waited for; matrix products, arithmetic and copies ran while one was open for 6% of the time, Pallas kernels for 0%

commit v1 on v0

v1 whole, which is shorter than its diff:
```python
import jax
import jax.numpy as jnp
from jax import lax
from jax.experimental import pallas as pl
from jax.experimental.pallas import tpu as pltpu
from jax.sharding import PartitionSpec as P

MESH = pl.DeviceIdType.MESH
BF = jnp.bfloat16
F32 = jnp.float32

SLABS = 5
RS = 16
W = 640
H = 256
CH = 64
HALF = 32

A_A, A_B, A_D = 0, 3, 6
R_R, R_L = 10, 14
G_R, G_L = 18, 22
S_D, S_B, S_A = 26, 27, 30
NSEM = 33


def enc4(v):
    t = v * jnp.abs(v) * (2.0**40)
    return (t * jnp.abs(t)).astype(BF)


def dec4(w):
    w = w.astype(F32)
    a = jnp.maximum(jnp.abs(w), 1e-37)
    r = lax.rsqrt(a)
    return (w * r) * (lax.rsqrt(a * r) * (2.0**-20))


def enc2(v):
    return (v * jnp.abs(v)).astype(BF)


def dec2(w):
    w = w.astype(F32)
    return w * lax.rsqrt(jnp.maximum(jnp.abs(w), 1e-37))


def kernel(
    tok_hbm, cot_hbm, wg_hbm, wu_hbm, wd_hbm,
    gtok_hbm, gwg_hbm, gwu_hbm, gwd_hbm,
    own, xy, wgu, wd, part, rsend, rrecv, hid, gx, dsend, drecv, bsend, brecv, asend, arecv,
    gtok, gwgu, gwd,
    ssem, rsem, lsem,
):
    r = lax.axis_index("row")
    c = lax.axis_index("col")
    core = lax.rem(c, 2)
    x = lax.rem(lax.div(c, 2), 4)
    y = lax.div(c, 8)
    a = x + core * (y - x)
    b = y + core * (x - y)

    def col(a_, b_):
        x_ = a_ + core * (b_ - a_)
        y_ = b_ + core * (a_ - b_)
        return y_ * 8 + x_ * 2 + core

    def m4(v):
        return lax.rem(v + 8, 4)

    def m8(v):
        return lax.rem(v + 16, 8)

    right = (m8(r + 1), c)
    left = (m8(r - 1), c)
    peer = (r, c + 1 - 2 * core)
    adev = {d: (r, col(m4(a + d), b)) for d in (1, 2, 3)}
    bdev = {d: (r, col(a, m4(b + d))) for d in (1, 2, 3)}

    loads = [
        pltpu.make_async_copy(tok_hbm, own.at[0], lsem.at[0]),
        pltpu.make_async_copy(cot_hbm, own.at[1], lsem.at[1]),
        pltpu.make_async_copy(wg_hbm, wgu.at[:, pl.ds(0, H)], lsem.at[2]),
        pltpu.make_async_copy(wu_hbm, wgu.at[:, pl.ds(H, H)], lsem.at[3]),
        pltpu.make_async_copy(wd_hbm, wd, lsem.at[4]),
    ]
    for cp in loads:
        cp.start()

    barrier = pltpu.get_barrier_semaphore()
    partners = [right, left, peer] + [adev[d] for d in (1, 2, 3)] + [bdev[d] for d in (1, 2, 3)]
    for dev in partners:
        pl.semaphore_signal(barrier, inc=1, device_id=dev, device_id_type=MESH)
    pl.semaphore_wait(barrier, len(partners))

    sent = []

    def copy(src, dst, s, k, dev):
        return pltpu.make_async_remote_copy(
            src_ref=src, dst_ref=dst, send_sem=ssem.at[s, k], recv_sem=rsem.at[s, k],
            device_id=dev, device_id_type=MESH,
        )

    def send(src, dst, s, k, dev):
        cp = copy(src, dst, s, k, dev)
        cp.start()
        sent.append(cp)

    def recv(dst, s, k):
        copy(dst, dst, s, k, right).wait_recv()

    def pos(s, co, b_, a_):
        return xy.at[s, pl.ds(co * 16 + b_ * 4 + a_, 1)]

    def line(s, co, b_):
        return xy.at[s, pl.ds(co * 16 + b_ * 4, 4)]

    def chunk(ref, s, j, lo=0, n=CH):
        return ref.at[s, pl.ds(pl.multiple_of(j * CH + lo, 32), n)]

    def gather0(s):
        me = pos(s, core, b, a)
        for d in (1, 2, 3):
            send(me, me, s, A_A + d - 1, adev[d])

    def gather1(s):
        for d in (1, 2, 3):
            recv(pos(s, core, b, m4(a - d)), s, A_A + d - 1)
        row = line(s, core, b)
        for d in (1, 2, 3):
            send(row, row, s, A_B + d - 1, bdev[d])
        send(row, row, s, A_D, peer)

    def gather2(s):
        for d in (1, 3, 2):
            row = line(s, core, m4(b - d))
            recv(row, s, A_B + d - 1)
            send(row, row, s, A_D + d, peer)

    def project(s):
        for d in range(4):
            recv(line(s, 1 - core, m4(a - d)), s, A_D + d)
        xs = xy[s, :, 0].reshape(32 * RS, W)
        ys = xy[s, :, 1].reshape(32 * RS, W)
        part[s, :, 0 : 2 * H] = jnp.dot(xs, wgu[...], preferred_element_type=F32)
        part[s, :, 2 * H : 3 * H] = lax.dot_general(
            ys, wd[...], (((1,), (1,)), ((), ())), preferred_element_type=F32
        )

    def reduce_step(s, h):
        if h == 0:
            far = m8(r + 4)
            rsend[s, 0, 0, 0:HALF] = enc4(chunk(part, s, far, 0, HALF)[...])
            rsend[s, 1, 0, 0:HALF] = enc4(chunk(part, s, far, HALF, HALF)[...])
            for way, dev, k in ((0, right, R_R), (1, left, R_L)):
                send(
                    rsend.at[s, way, 0, pl.ds(0, HALF)],
                    rrecv.at[s, way, 0, pl.ds(0, HALF)],
                    s, k, dev,
                )
            return
        for way, dev, k, j in ((0, right, R_R, m8(r + 4 - h)), (1, left, R_L, m8(r - 4 + h))):
            if h == 1:
                got = rrecv.at[s, way, 0, pl.ds(0, HALF)]
                recv(got, s, k)
                near, rest = (0, HALF) if way == 0 else (HALF, 0)
                rsend[s, way, 1, near : near + HALF] = enc4(
                    chunk(part, s, j, near, HALF)[...] + dec4(got[...])
                )
                rsend[s, way, 1, rest : rest + HALF] = enc4(chunk(part, s, j, rest, HALF)[...])
            else:
                got = rrecv.at[s, way, h - 1]
                recv(got, s, k + h - 1)
                rsend[s, way, h] = enc4(chunk(part, s, j)[...] + dec4(got[...]))
            send(rsend.at[s, way, h], rrecv.at[s, way, h], s, k + h, dev)

    def activate(s):
        recv(rrecv.at[s, 0, 3], s, R_R + 3)
        recv(rrecv.at[s, 1, 3], s, R_L + 3)
        mine = chunk(part, s, r)
        total = mine[...] + dec4(rrecv[s, 0, 3]) + dec4(rrecv[s, 1, 3])
        g, u, gh = total[:, 0:H], total[:, H : 2 * H], total[:, 2 * H :]
        sg = jax.nn.sigmoid(g)
        silu = g * sg
        out = chunk(hid, s, r)
        out[:, 0:H] = (gh * u * sg * (1.0 + g * (1.0 - sg))).astype(BF)
        out[:, H : 2 * H] = (gh * silu).astype(BF)
        out[:, 2 * H :] = (silu * u).astype(BF)

    def spread_step(s, h):
        if h == 0:
            mine = chunk(hid, s, r)
            send(mine, mine, s, G_R, right)
            send(mine, mine, s, G_L, left)
            return
        if h <= 3:
            lo, hi = chunk(hid, s, m8(r - h)), chunk(hid, s, m8(r + h))
            recv(lo, s, G_R + h - 1)
            if h == 3:
                half = chunk(hid, s, m8(r - 3), 0, HALF)
                send(half, half, s, G_R + 3, right)
            else:
                send(lo, lo, s, G_R + h, right)
            recv(hi, s, G_L + h - 1)
            if h == 3:
                half = chunk(hid, s, m8(r + 3), HALF, HALF)
                send(half, half, s, G_L + 3, left)
            else:
                send(hi, hi, s, G_L + h, left)
            return
        recv(chunk(hid, s, m8(r + 4), 0, HALF), s, G_R + 3)
        recv(chunk(hid, s, m8(r + 4), HALF, HALF), s, G_L + 3)

    def token_grad(s):
        gx[...] = lax.dot_general(
            hid[s, :, 0 : 2 * H], wgu[...], (((1,), (1,)), ((), ())), preferred_element_type=F32
        )
        theirs = pl.ds(pl.multiple_of((1 - core) * 256, 256), 256)
        dsend[s] = enc2(gx[theirs])
        send(dsend.at[s], drecv.at[s], s, S_D, peer)

    def weight_grads(s):
        xs = xy[s, :, 0].reshape(32 * RS, W)
        ys = xy[s, :, 1].reshape(32 * RS, W)
        over = (((0,), (0,)), ((), ()))
        dgu = lax.dot_general(xs, hid[s, :, 0 : 2 * H], over, preferred_element_type=F32)
        dd = lax.dot_general(hid[s, :, 2 * H :], ys, over, preferred_element_type=F32)
        if s == 0:
            gwgu[...] = dgu
            gwd[...] = dd
        else:
            gwgu[...] += dgu
            gwd[...] += dd

    def scatter1(s):
        recv(drecv.at[s], s, S_D)
        gx[0:256] = gx[pl.ds(pl.multiple_of(core * 256, 256), 256)] + dec2(drecv[s])
        for d in (1, 2, 3):
            rows = pl.ds(pl.multiple_of(m4(b + d) * CH, CH), CH)
            bsend[s, d - 1] = enc2(gx[rows])
            send(bsend.at[s, d - 1], brecv.at[s, d - 1], s, S_B + d - 1, bdev[d])

    def scatter2(s):
        total = gx[pl.ds(pl.multiple_of(b * CH, CH), CH)]
        for d in (1, 2, 3):
            recv(brecv.at[s, d - 1], s, S_B + d - 1)
            total = total + dec2(brecv[s, d - 1])
        gx[0:CH] = total
        for d in (1, 2, 3):
            rows = pl.ds(pl.multiple_of(m4(a + d) * RS, RS), RS)
            asend[s, d - 1] = enc2(gx[rows])
            send(asend.at[s, d - 1], arecv.at[s, d - 1], s, S_A + d - 1, adev[d])
        gtok[s * RS : (s + 1) * RS] = gx[pl.ds(pl.multiple_of(a * RS, RS), RS)]

    def scatter3(s):
        total = gtok[s * RS : (s + 1) * RS]
        for d in (1, 2, 3):
            recv(arecv.at[s, d - 1], s, S_A + d - 1)
            total = total + dec2(arecv[s, d - 1])
        gtok[s * RS : (s + 1) * RS] = total

    def place_own():
        loads[0].wait()
        loads[1].wait()
        for s in range(SLABS):
            for k in range(2):
                xy[s, pl.ds(core * 16 + b * 4 + a, 1), k] = own[k, s * RS : (s + 1) * RS][None]

    def wait_weights():
        for cp in loads[2:]:
            cp.wait()

    tasks = [(-20.0, place_own), (-0.6, wait_weights)]
    for s in range(SLABS):
        t = 2.0 * s
        tasks.append((t - 12 if s < 2 else t - 3.5, lambda s=s: gather0(s)))
        tasks.append((t - 2.4, lambda s=s: gather1(s)))
        tasks.append((t - 1.4, lambda s=s: gather2(s)))
        tasks.append((t - 0.4, lambda s=s: project(s)))
        for h in range(4):
            tasks.append((t + h, lambda s=s, h=h: reduce_step(s, h)))
        tasks.append((t + 4, lambda s=s: activate(s)))
        for h in range(5):
            tasks.append((t + 4.1 + h, lambda s=s, h=h: spread_step(s, h)))
        tasks.append((t + 8.2, lambda s=s: token_grad(s)))
        tasks.append((t + 8.3, lambda s=s: weight_grads(s)))
        tasks.append((t + 8.7, lambda s=s: scatter1(s)))
        tasks.append((t + 9.7, lambda s=s: scatter2(s)))
        tasks.append((t + 11.3, lambda s=s: scatter3(s)))
    for _, task in sorted(tasks, key=lambda p: p[0]):
        task()

    stores = [
        pltpu.make_async_copy(gtok, gtok_hbm, lsem.at[0]),
        pltpu.make_async_copy(gwgu.at[:, pl.ds(0, H)], gwg_hbm, lsem.at[1]),
        pltpu.make_async_copy(gwgu.at[:, pl.ds(H, H)], gwu_hbm, lsem.at[2]),
        pltpu.make_async_copy(gwd, gwd_hbm, lsem.at[3]),
    ]
    for cp in stores:
        cp.start()
    for cp in sent:
        cp.wait_send()
    for cp in stores:
        cp.wait()


def per_device(tokens, cotangent, gate_weight, up_weight, down_weight):
    hbm = pl.BlockSpec(memory_space=pl.ANY)
    rows = 32 * RS
    vm = pltpu.VMEM
    return pl.pallas_call(
        kernel,
        out_shape=(
            jax.ShapeDtypeStruct((SLABS * RS, W), F32),
            jax.ShapeDtypeStruct((W, H), F32),
            jax.ShapeDtypeStruct((W, H), F32),
            jax.ShapeDtypeStruct((H, W), F32),
        ),
        in_specs=[hbm] * 5,
        out_specs=[hbm] * 4,
        scratch_shapes=[
            vm((2, SLABS * RS, W), BF),
            vm((SLABS, 32, 2, RS, W), BF),
            vm((W, 2 * H), BF),
            vm((H, W), BF),
            vm((SLABS, rows, 3 * H), F32),
            vm((SLABS, 2, 4, CH, 3 * H), BF),
            vm((SLABS, 2, 4, CH, 3 * H), BF),
            vm((SLABS, rows, 3 * H), BF),
            vm((rows, W), F32),
            vm((SLABS, 256, W), BF),
            vm((SLABS, 256, W), BF),
            vm((SLABS, 3, CH, W), BF),
            vm((SLABS, 3, CH, W), BF),
            vm((SLABS, 3, RS, W), BF),
            vm((SLABS, 3, RS, W), BF),
            vm((SLABS * RS, W), F32),
            vm((W, 2 * H), F32),
            vm((H, W), F32),
            pltpu.SemaphoreType.DMA((SLABS, NSEM)),
            pltpu.SemaphoreType.DMA((SLABS, NSEM)),
            pltpu.SemaphoreType.DMA((5,)),
        ],
        compiler_params=pltpu.CompilerParams(
            collective_id=0, has_side_effects=True, vmem_limit_bytes=58 * 2**20
        ),
        name="swiglu_backward",
    )(tokens, cotangent, gate_weight, up_weight, down_weight)


def solution(mesh):
    in_specs = (P("col", "row"), P("col", "row"), P("row", "col"), P("row", "col"), P("col", "row"))
    out_specs = (P("col", "row"), P("row", "col"), P("row", "col"), P("col", "row"))
    return jax.shard_map(
        per_device, mesh=mesh, in_specs=in_specs, out_specs=out_specs, check_vma=False
    )
```

time: 409 us -> 139 us (0.34)
  waiting for transfers between devices: 356 us -> 0 us
  Pallas kernels: 0 us -> 133 us
  matrix products: 30.4 us -> 0 us
  between operations: 13.8 us -> 0.64 us
  other arithmetic: 4.5 us -> 0 us
    psum x1 -> x0, waiting for transfers between devices: 178 us -> none  [per_device(): gate_proj, up_proj = lax.psum((gate_proj, up_proj), 'row')]
    pallas_call x0 -> x1, Pallas kernels: none -> 133 us  [per_device(): pl.pallas_call(kernel, out_shape=(jax.ShapeDtypeStruct((SLABS * RS, W), F...]
    all_gather x2 -> x0, waiting for transfers between devices: 101 us -> none  [the longest x1 56.5 us: per_device(): tok_rows = lax.all_gather(tokens, 'col', axis=0, tiled=True)]
    reduce_scatter x1 -> x0, waiting for transfers between devices: 75.3 us -> none  [per_device(): lax.psum_scatter(result + lax.dot_general(grad_up, up_weight, contract_co...]
    dot_general x8 -> x0, matrix products: 30.4 us -> none  [the longest x1 5.89 us: per_device(): lax.dot_general(hidden, cot_rows, contract_rows, preferred_element_type=j...]
    convert_element_type x1 -> x0, other arithmetic: 4.5 us -> none  [swiglu_backward(): grad_up = (grad_hidden * silu_gate).astype(jnp.bfloat16)]
  transfers between devices with their start and end apart: 4 -> 0, of which waited for: 4 -> 0; matrix products, arithmetic and copies ran while one was open for 6% -> 0% of each run, Pallas kernels for 0% -> 0%
where the time goes in v1:
time: 139 us
  Pallas kernels  133 us (96%)
  local copies, waits for them, and re-layouts  5.82 us (4%)
    pallas_call x1, Pallas kernels, per_device(): pl.pallas_call(kernel, out_shape=(jax.ShapeDtypeStruct((SLABS * RS, W), F...  133 us
    unnamed x8, local copies, waits for them, and re-layouts  5.82 us

profile of v1, /device:TPU:1, one launch (start us, length us, event | category | flops | bytes accessed | tf_op | source)
XLA Modules:
  0.0 139.2 jit_solution(4904748044458477874)
XLA Ops:
  0.6 132.7 %swiglu_backward.1 = (f32[80,640]{1,0:T(8,128)}, f32[640,256]{1,0:T(8,128)}, f32[640,256]{1,0:T(8,128)}, f32[256,640]{1,0:T(8,128)}) custom-call(bf16[80,640]{1,0:T(8,128)(2,1)} %tok_hbm.1, bf16[80,640]{1,0:T(8,128)(2,1)} %cot_hbm.1, bf16[640,256]{1,0:T(8,128)(2,1)} %wg_hbm.1, bf16[640,256]{1,0:T(8,128)(2,1)} %wu_hbm.1, bf16[256,640]{1,0:T(8,128)(2,1)} %wd_hbm.1), custom_call_target="tpu_custom_call" | custom-call | tf_op jit(solution)/shard_map/swiglu_backward/pallas_call | solution.py:310
  133.4 1.6 %copy.13 = f32[80,640]{1,0:T(8,128)} copy(f32[80,640]{1,0:T(8,128)} %get-tuple-element.8) | data formatting | bytes 409600
  135.0 0.0 copy-start.1
  135.0 2.0 %copy.14 = f32[640,256]{1,0:T(8,128)} copy(f32[640,256]{1,0:T(8,128)} %get-tuple-element.9) | data formatting | bytes 1310720
  137.0 0.0 copy-done.1
  137.0 0.0 copy-start
  137.0 0.8 copy.15
  137.9 0.5 copy-done
  138.4 0.8 copy.16
Async XLA Ops:
  135.0 2.0 %copy-start.1 = (f32[640,256]{1,0:T(8,128)S(1)}, f32[640,256]{1,0:T(8,128)}, u32[]{:S(2)}) copy-start(f32[640,256]{1,0:T(8,128)} %get-tuple-element.10) | copy-start | bytes 1966084
  137.0 1.3 copy-start

commit v2 on v1

v2 whole, which is shorter than its diff:
```python
import jax
import jax.numpy as jnp
from jax import lax
from jax.experimental import pallas as pl
from jax.experimental.pallas import tpu as pltpu
from jax.sharding import PartitionSpec as P

MESH = pl.DeviceIdType.MESH
BF = jnp.bfloat16
F32 = jnp.float32

SLABS = 5
RS = 16
W = 640
H = 256
CH = 64
HALF = 32

FH = 128
ZW = 3 * FH

A_A, A_B, A_D = 0, 3, 6
S_D, S_B, S_A = 10, 14, 17
R_R, R_L = 20, 28
G_R, G_L = 36, 44
NSEM = 52


def enc4(v):
    t = v * jnp.abs(v) * (2.0**40)
    return (t * jnp.abs(t)).astype(BF)


def dec4(w):
    w = w.astype(F32)
    a = jnp.maximum(jnp.abs(w), 1e-37)
    r = lax.rsqrt(a)
    return (w * r) * (lax.rsqrt(a * r) * (2.0**-20))


def enc2(v):
    return (v * jnp.abs(v)).astype(BF)


def dec2(w):
    w = w.astype(F32)
    return w * lax.rsqrt(jnp.maximum(jnp.abs(w), 1e-37))


ORDER = (
    ("g0", 0), ("g0", 1), ("g1", 0), ("g1", 1), ("g2", 0), ("g0", 2), ("g0", 3), ("pj", 0, 0),
    ("r0", 0, 0), ("pj", 0, 1), ("r0", 0, 1), ("g2", 1), ("g0", 4), ("r1", 0, 0), ("g1", 2),
    ("r1", 0, 1), ("pj", 1, 0), ("r0", 1, 0), ("pj", 1, 1), ("r0", 1, 1), ("r2", 0, 0),
    ("r2", 0, 1), ("r1", 1, 0), ("g1", 3), ("g1", 4), ("r1", 1, 1), ("r3", 0, 0), ("g2", 2),
    ("r3", 0, 1), ("r2", 1, 0), ("r2", 1, 1), ("h0", 0, 0), ("h0", 0, 1), ("r3", 1, 0),
    ("pj", 2, 0), ("r3", 1, 1), ("r0", 2, 0), ("g2", 3), ("pj", 2, 1), ("h1", 0, 0),
    ("h1", 0, 1), ("h0", 1, 1), ("h0", 1, 0), ("pj", 3, 0), ("pj", 3, 1), ("h2", 0, 0),
    ("r0", 2, 1), ("r0", 3, 1), ("g2", 4), ("r0", 3, 0), ("r1", 2, 0), ("h1", 1, 1),
    ("r1", 3, 1), ("h1", 1, 0), ("r1", 2, 1), ("h2", 0, 1), ("r1", 3, 0), ("h2", 1, 0),
    ("r2", 2, 0), ("r2", 2, 1), ("pj", 4, 0), ("h2", 1, 1), ("tA", 1), ("pj", 4, 1), ("tA", 0),
    ("h3", 0, 0), ("uA", 0), ("r0", 4, 1), ("h3", 0, 1), ("r3", 2, 0), ("h3", 1, 1),
    ("h4", 0, 0), ("r2", 3, 0), ("r3", 2, 1), ("r1", 4, 1), ("h3", 1, 0), ("h0", 2, 0),
    ("h4", 1, 1), ("uA", 1), ("tB", 0), ("r2", 3, 1), ("r0", 4, 0), ("h4", 0, 1), ("r3", 3, 0),
    ("h0", 2, 1), ("uB", 0), ("tC", 0), ("r2", 4, 1), ("uC", 0), ("r1", 4, 0), ("h1", 2, 0),
    ("h1", 2, 1), ("r3", 3, 1), ("tB", 1), ("wg", 0), ("r3", 4, 1), ("s2", 0), ("h2", 2, 0),
    ("h2", 2, 1), ("h4", 1, 0), ("uB", 1), ("h0", 3, 0), ("tC", 1), ("r2", 4, 0), ("uC", 1),
    ("h0", 3, 1), ("h3", 2, 0), ("h3", 2, 1), ("wg", 1), ("h1", 3, 0), ("tA", 2), ("r3", 4, 0),
    ("tB", 2), ("h4", 2, 0), ("h0", 4, 1), ("h1", 3, 1), ("uA", 2), ("uB", 2), ("h2", 3, 0),
    ("h4", 2, 1), ("tC", 2), ("s2", 1), ("h0", 4, 0), ("h2", 3, 1), ("h1", 4, 1), ("uC", 2),
    ("tA", 3), ("h1", 4, 0), ("h3", 3, 0), ("h3", 3, 1), ("uA", 3), ("s3", 0), ("h2", 4, 1),
    ("tB", 3), ("h2", 4, 0), ("s2", 2), ("tA", 4), ("h4", 3, 1), ("h4", 3, 0), ("uB", 3),
    ("h3", 4, 1), ("tC", 3), ("uA", 4), ("h3", 4, 0), ("tB", 4), ("uC", 3), ("wg", 2),
    ("h4", 4, 1), ("h4", 4, 0), ("uB", 4), ("tC", 4), ("uC", 4), ("wg", 3), ("s3", 1),
    ("s2", 3), ("s2", 4), ("s3", 3), ("wg", 4), ("s3", 2), ("s3", 4),
)


def kernel(
    tok_hbm, cot_hbm, wg_hbm, wu_hbm, wd_hbm,
    gtok_hbm, gwg_hbm, gwu_hbm, gwd_hbm,
    xy, wgu, wd, part, rsend, rrecv, hid, gx, keep, dsend, drecv, bsend, brecv, asend, arecv,
    gtok, gwgu, gwd,
    ssem, rsem, lsem,
):
    r = lax.axis_index("row")
    c = lax.axis_index("col")
    core = lax.rem(c, 2)
    x = lax.rem(lax.div(c, 2), 4)
    y = lax.div(c, 8)
    a = x + core * (y - x)
    b = y + core * (x - y)

    def col(a_, b_):
        x_ = a_ + core * (b_ - a_)
        y_ = b_ + core * (a_ - b_)
        return y_ * 8 + x_ * 2 + core

    def m4(v):
        return lax.rem(v + 8, 4)

    def m8(v):
        return lax.rem(v + 16, 8)

    right = (m8(r + 1), c)
    left = (m8(r - 1), c)
    peer = (r, c + 1 - 2 * core)
    adev = {d: (r, col(m4(a + d), b)) for d in (1, 2, 3)}
    bdev = {d: (r, col(a, m4(b + d))) for d in (1, 2, 3)}
    place = core * 16 + b * 4 + a

    own_loads = [
        [
            pltpu.make_async_copy(
                src.at[pl.ds(s * RS, RS)], xy.at[s, place, k], lsem.at[2 * s + k]
            )
            for k, src in enumerate((tok_hbm, cot_hbm))
        ]
        for s in range(SLABS)
    ]
    weight_loads = [pltpu.make_async_copy(wd_hbm, wd, lsem.at[10])]
    for f in range(2):
        for k, src in enumerate((wg_hbm, wu_hbm)):
            weight_loads.append(
                pltpu.make_async_copy(
                    src.at[:, pl.ds(f * FH, FH)],
                    wgu.at[:, pl.ds((2 * f + k) * FH, FH)],
                    lsem.at[11 + 2 * f + k],
                )
            )
    for cp in sum(own_loads, []) + weight_loads:
        cp.start()

    barrier = pltpu.get_barrier_semaphore()
    partners = [right, left, peer] + [adev[d] for d in (1, 2, 3)] + [bdev[d] for d in (1, 2, 3)]
    for dev in partners:
        pl.semaphore_signal(barrier, inc=1, device_id=dev, device_id_type=MESH)
    pl.semaphore_wait(barrier, len(partners))

    sent = []

    def copy(src, dst, s, k, dev):
        return pltpu.make_async_remote_copy(
            src_ref=src, dst_ref=dst, send_sem=ssem.at[s, k], recv_sem=rsem.at[s, k],
            device_id=dev, device_id_type=MESH,
        )

    def send(src, dst, s, k, dev):
        cp = copy(src, dst, s, k, dev)
        cp.start()
        sent.append(cp)

    def recv(dst, s, k):
        copy(dst, dst, s, k, right).wait_recv()

    def pos(s, co, b_, a_):
        return xy.at[s, pl.ds(co * 16 + b_ * 4 + a_, 1)]

    def line(s, co, b_):
        return xy.at[s, pl.ds(co * 16 + b_ * 4, 4)]

    def chunk(ref, z, j, lo=0, n=CH):
        return ref.at[z, pl.ds(pl.multiple_of(j * CH + lo, 32), n)]

    def gather0(s):
        for cp in own_loads[s]:
            cp.wait()
        me = pos(s, core, b, a)
        for d in (1, 2, 3):
            send(me, me, s, A_A + d - 1, adev[d])

    def gather1(s):
        for d in (1, 2, 3):
            recv(pos(s, core, b, m4(a - d)), s, A_A + d - 1)
        row = line(s, core, b)
        for d in (1, 2, 3):
            send(row, row, s, A_B + d - 1, bdev[d])
        send(row, row, s, A_D, peer)

    def gather2(s):
        for d in (1, 3, 2):
            row = line(s, core, m4(b - d))
            recv(row, s, A_B + d - 1)
            send(row, row, s, A_D + d, peer)

    def project(s, f):
        z = 2 * s + f
        if f == 0:
            for d in range(4):
                recv(line(s, 1 - core, m4(a - d)), s, A_D + d)
            if s == 0:
                for cp in weight_loads:
                    cp.wait()
        xs = xy[s, :, 0].reshape(32 * RS, W)
        ys = xy[s, :, 1].reshape(32 * RS, W)
        part[z, :, 0 : 2 * FH] = jnp.dot(
            xs, wgu[:, 2 * FH * f : 2 * FH * (f + 1)], preferred_element_type=F32
        )
        part[z, :, 2 * FH : ZW] = lax.dot_general(
            ys, wd[FH * f : FH * (f + 1)], (((1,), (1,)), ((), ())), preferred_element_type=F32
        )

    def reduce_step(s, f, h):
        z = 2 * s + f
        kr, kl = R_R + 4 * f, R_L + 4 * f
        if h == 0:
            far = m8(r + 4)
            rsend[z, 0, 0, 0:HALF] = enc4(chunk(part, z, far, 0, HALF)[...])
            rsend[z, 1, 0, 0:HALF] = enc4(chunk(part, z, far, HALF, HALF)[...])
            for way, dev, k in ((0, right, kr), (1, left, kl)):
                send(
                    rsend.at[z, way, 0, pl.ds(0, HALF)],
                    rrecv.at[z, way, 0, pl.ds(0, HALF)],
                    s, k, dev,
                )
            return
        for way, dev, k, j in ((0, right, kr, m8(r + 4 - h)), (1, left, kl, m8(r - 4 + h))):
            if h == 1:
                got = rrecv.at[z, way, 0, pl.ds(0, HALF)]
                recv(got, s, k)
                near, rest = (0, HALF) if way == 0 else (HALF, 0)
                rsend[z, way, 1, near : near + HALF] = enc4(
                    chunk(part, z, j, near, HALF)[...] + dec4(got[...])
                )
                rsend[z, way, 1, rest : rest + HALF] = enc4(chunk(part, z, j, rest, HALF)[...])
            else:
                got = rrecv.at[z, way, h - 1]
                recv(got, s, k + h - 1)
                rsend[z, way, h] = enc4(chunk(part, z, j)[...] + dec4(got[...]))
            send(rsend.at[z, way, h], rrecv.at[z, way, h], s, k + h, dev)

    def activate(s, f):
        z = 2 * s + f
        recv(rrecv.at[z, 0, 3], s, R_R + 4 * f + 3)
        recv(rrecv.at[z, 1, 3], s, R_L + 4 * f + 3)
        mine = chunk(part, z, r)
        total = mine[...] + dec4(rrecv[z, 0, 3]) + dec4(rrecv[z, 1, 3])
        g, u, gh = total[:, 0:FH], total[:, FH : 2 * FH], total[:, 2 * FH :]
        sg = jax.nn.sigmoid(g)
        silu = g * sg
        out = chunk(hid, z, r)
        out[:, 0:FH] = (gh * u * sg * (1.0 + g * (1.0 - sg))).astype(BF)
        out[:, FH : 2 * FH] = (gh * silu).astype(BF)
        out[:, 2 * FH :] = (silu * u).astype(BF)

    def spread_step(s, f, h):
        z = 2 * s + f
        kr, kl = G_R + 4 * f, G_L + 4 * f
        if h == 0:
            activate(s, f)
            mine = chunk(hid, z, r)
            send(mine, mine, s, kr, right)
            send(mine, mine, s, kl, left)
            return
        if h <= 3:
            lo, hi = chunk(hid, z, m8(r - h)), chunk(hid, z, m8(r + h))
            recv(lo, s, kr + h - 1)
            if h == 3:
                half = chunk(hid, z, m8(r - 3), 0, HALF)
                send(half, half, s, kr + 3, right)
            else:
                send(lo, lo, s, kr + h, right)
            recv(hi, s, kl + h - 1)
            if h == 3:
                half = chunk(hid, z, m8(r + 3), HALF, HALF)
                send(half, half, s, kl + 3, left)
            else:
                send(hi, hi, s, kl + h, left)
            return
        recv(chunk(hid, z, m8(r + 4), 0, HALF), s, kr + 3)
        recv(chunk(hid, z, m8(r + 4), HALF, HALF), s, kl + 3)

    order = [m4(r + 2), m4(r + 1), m4(r + 3), m4(r)]

    def token_grad(s, i):
        def rows_of(co):
            j = co * 4 + order[i]
            both = [chunk(hid, 2 * s + f, j)[:, 0 : 2 * FH] for f in range(2)]
            return lax.dot_general(
                jnp.concatenate(both, axis=1), wgu[...], (((1,), (1,)), ((), ())),
                preferred_element_type=F32,
            )

        dsend[s, i] = enc2(rows_of(1 - core))
        send(dsend.at[s, i], drecv.at[s, i], s, S_D + i, peer)
        gx[s % 2, i] = rows_of(core)

    def add_peer(s, i):
        recv(drecv.at[s, i], s, S_D + i)
        total = gx[s % 2, i] + dec2(drecv[s, i])
        d = m4(order[i] - b)

        @pl.when(d == 0)
        def _():
            keep[s % 2] = total

        @pl.when(d != 0)
        def _():
            bsend[s, i] = enc2(total)
            copy(
                bsend.at[s, i], brecv.at[s, d - 1], s, S_B + d - 1, (r, col(a, order[i]))
            ).start()

    def weight_grads(s):
        xs = xy[s, :, 0].reshape(32 * RS, W)
        ys = xy[s, :, 1].reshape(32 * RS, W)
        over = (((0,), (0,)), ((), ()))
        gu = jnp.concatenate([hid[2 * s + f, :, 0 : 2 * FH] for f in range(2)], axis=1)
        hd = jnp.concatenate([hid[2 * s + f, :, 2 * FH :] for f in range(2)], axis=1)
        dgu = lax.dot_general(xs, gu, over, preferred_element_type=F32)
        dd = lax.dot_general(hd, ys, over, preferred_element_type=F32)
        if s == 0:
            gwgu[...] = dgu
            gwd[...] = dd
        else:
            gwgu[...] += dgu
            gwd[...] += dd

    def scatter2(s):
        total = keep[s % 2]
        for d in (1, 2, 3):
            recv(brecv.at[s, d - 1], s, S_B + d - 1)
            total = total + dec2(brecv[s, d - 1])
        keep[s % 2] = total
        for d in (1, 2, 3):
            rows = pl.ds(pl.multiple_of(m4(a + d) * RS, RS), RS)
            asend[s, d - 1] = enc2(keep[s % 2, rows])
            send(asend.at[s, d - 1], arecv.at[s, d - 1], s, S_A + d - 1, adev[d])
        gtok[s * RS : (s + 1) * RS] = keep[s % 2, pl.ds(pl.multiple_of(a * RS, RS), RS)]

    def scatter3(s):
        total = gtok[s * RS : (s + 1) * RS]
        for d in (1, 2, 3):
            recv(arecv.at[s, d - 1], s, S_A + d - 1)
            total = total + dec2(arecv[s, d - 1])
        gtok[s * RS : (s + 1) * RS] = total

    def run(name, s, f=0):
        if name[0] == "r":
            reduce_step(s, f, int(name[1]))
        elif name[0] == "h":
            spread_step(s, f, int(name[1]))
        elif name[0] == "t":
            for i in {"A": (0,), "B": (1, 2), "C": (3,)}[name[1]]:
                token_grad(s, i)
        elif name[0] == "u":
            for i in {"A": (0,), "B": (1, 2), "C": (3,)}[name[1]]:
                add_peer(s, i)
        elif name == "pj":
            project(s, f)
        else:
            {
                "g0": gather0, "g1": gather1, "g2": gather2,
                "wg": weight_grads, "s2": scatter2, "s3": scatter3,
            }[name](s)

    for step in ORDER:
        run(*step)

    stores = [
        pltpu.make_async_copy(gtok, gtok_hbm, lsem.at[0]),
        pltpu.make_async_copy(gwd, gwd_hbm, lsem.at[1]),
    ]
    for f in range(2):
        for k, dst in enumerate((gwg_hbm, gwu_hbm)):
            stores.append(
                pltpu.make_async_copy(
                    gwgu.at[:, pl.ds((2 * f + k) * FH, FH)],
                    dst.at[:, pl.ds(f * FH, FH)],
                    lsem.at[2 + 2 * f + k],
                )
            )
    for cp in stores:
        cp.start()
    for cp in sent:
        cp.wait_send()
    for s in range(SLABS):
        for d in (1, 2, 3):
            copy(bsend.at[s, 0], brecv.at[s, d - 1], s, S_B + d - 1, bdev[d]).wait_send()
    for cp in stores:
        cp.wait()


def write_out(*refs):
    ins, outs, bufs, sem_in, sem_out = refs[0:4], refs[4:8], refs[8:12], refs[12], refs[13]
    reads, writes = [], []
    for k, (src, buf, dst) in enumerate(zip(ins, bufs, outs)):
        n = src.shape[0] // 2
        for i in range(2):
            rows = pl.ds(i * n, n)
            reads.append(pltpu.make_async_copy(src.at[rows], buf.at[rows], sem_in.at[2 * k + i]))
            writes.append(pltpu.make_async_copy(buf.at[rows], dst.at[rows], sem_out.at[2 * k + i]))
    for cp in reads:
        cp.start()
    for rd, wr in zip(reads, writes):
        rd.wait()
        wr.start()
    for wr in writes:
        wr.wait()


def per_device(tokens, cotangent, gate_weight, up_weight, down_weight):
    hbm = pl.BlockSpec(memory_space=pl.ANY)
    rows = 32 * RS
    vm = pltpu.VMEM
    outs = pl.pallas_call(
        kernel,
        out_shape=(
            jax.ShapeDtypeStruct((SLABS * RS, W), F32),
            jax.ShapeDtypeStruct((W, H), F32),
            jax.ShapeDtypeStruct((W, H), F32),
            jax.ShapeDtypeStruct((H, W), F32),
        ),
        in_specs=[hbm] * 5,
        out_specs=[hbm] * 4,
        scratch_shapes=[
            vm((SLABS, 32, 2, RS, W), BF),
            vm((W, 2 * H), BF),
            vm((H, W), BF),
            vm((2 * SLABS, rows, ZW), F32),
            vm((2 * SLABS, 2, 4, CH, ZW), BF),
            vm((2 * SLABS, 2, 4, CH, ZW), BF),
            vm((2 * SLABS, rows, ZW), BF),
            vm((2, 4, CH, W), F32),
            vm((2, CH, W), F32),
            vm((SLABS, 4, CH, W), BF),
            vm((SLABS, 4, CH, W), BF),
            vm((SLABS, 4, CH, W), BF),
            vm((SLABS, 3, CH, W), BF),
            vm((SLABS, 3, RS, W), BF),
            vm((SLABS, 3, RS, W), BF),
            vm((SLABS * RS, W), F32),
            vm((W, 2 * H), F32),
            vm((H, W), F32),
            pltpu.SemaphoreType.DMA((SLABS, NSEM)),
            pltpu.SemaphoreType.DMA((SLABS, NSEM)),
            pltpu.SemaphoreType.DMA((15,)),
        ],
        compiler_params=pltpu.CompilerParams(
            collective_id=0, has_side_effects=True, vmem_limit_bytes=61 * 2**20
        ),
        name="swiglu_backward",
    )(tokens, cotangent, gate_weight, up_weight, down_weight)
    return pl.pallas_call(
        write_out,
        out_shape=[jax.ShapeDtypeStruct(o.shape, o.dtype) for o in outs],
        in_specs=[hbm] * 4,
        out_specs=[hbm] * 4,
        scratch_shapes=[vm(o.shape, o.dtype) for o in outs]
        + [pltpu.SemaphoreType.DMA((8,)), pltpu.SemaphoreType.DMA((8,))],
        name="write_out",
    )(*outs)


def solution(mesh):
    in_specs = (P("col", "row"), P("col", "row"), P("row", "col"), P("row", "col"), P("col", "row"))
    out_specs = (P("col", "row"), P("row", "col"), P("row", "col"), P("col", "row"))
    return jax.shard_map(
        per_device, mesh=mesh, in_specs=in_specs, out_specs=out_specs, check_vma=False
    )
```

time: 139 us -> 125 us (0.90)
  Pallas kernels: 133 us -> 124 us
  local copies, waits for them, and re-layouts: 5.82 us -> 0 us
    pallas_call x1, Pallas kernels: 133 us -> 122 us  [per_device(): pl.pallas_call(kernel, out_shape=(jax.ShapeDtypeStruct((SLABS * RS, W), F...]
    unnamed x8 -> x0, local copies, waits for them, and re-layouts: 5.82 us -> none
    pallas_call x0 -> x1, Pallas kernels: none -> 2.48 us  [per_device(): pl.pallas_call(write_out, out_shape=[jax.ShapeDtypeStruct(o.shape, o.dtyp...]
where the time goes in v2:
time: 125 us
  Pallas kernels  124 us (99%)
    pallas_call x1, Pallas kernels, per_device(): pl.pallas_call(kernel, out_shape=(jax.ShapeDtypeStruct((SLABS * RS, W), F...  122 us

profile of v2, /device:TPU:1, one launch (start us, length us, event | category | flops | bytes accessed | tf_op | source)
XLA Modules:
  0.0 125.2 jit_solution(589793291173652303)
XLA Ops:
  0.6 121.9 %swiglu_backward.1 = (f32[80,640]{1,0:T(8,128)}, f32[640,256]{1,0:T(8,128)}, f32[640,256]{1,0:T(8,128)}, f32[256,640]{1,0:T(8,128)}) custom-call(bf16[80,640]{1,0:T(8,128)(2,1)} %tok_hbm.1, bf16[80,640]{1,0:T(8,128)(2,1)} %cot_hbm.1, bf16[640,256]{1,0:T(8,128)(2,1)} %wg_hbm.1, bf16[640,256]{1,0:T(8,128)(2,1)} %wu_hbm.1, bf16[256,640]{1,0:T(8,128)(2,1)} %wd_hbm.1), custom_call_target="tpu_custom_call" | custom-call | tf_op jit(solution)/shard_map/swiglu_backward/pallas_call | solution.py:405
  122.5 2.5 %write_out.1 = (f32[80,640]{1,0:T(8,128)}, f32[640,256]{1,0:T(8,128)}, f32[640,256]{1,0:T(8,128)}, f32[256,640]{1,0:T(8,128)}) custom-call(f32[80,640]{1,0:T(8,128)} %get-tuple-element.8.refs_0_, f32[640,256]{1,0:T(8,128)} %get-tuple-element.9.refs_1_, f32[640,256]{1,0:T(8,128)} %get-tuple-element.10.refs_2_, f32[256,640]{1,0:T(8,128)} %get-tuple-element.11.refs_3_), custom_call_target="tpu_custom_call" | custom-call | tf_op jit(solution)/shard_map/write_out/pallas_call | solution.py:443

commit v3 on v2

v3 whole, which is shorter than its diff:
```python
import jax
import jax.numpy as jnp
from jax import lax
from jax.experimental import pallas as pl
from jax.experimental.pallas import tpu as pltpu
from jax.sharding import PartitionSpec as P

MESH = pl.DeviceIdType.MESH
BF = jnp.bfloat16
F32 = jnp.float32

SLABS = 5
RS = 16
W = 640
H = 256
CH = 64
HALF = 32

ZW = 3 * H

SUM_PARTS = (((0, 2 * H), (2 * H, H)), ((0, 2 * H), (2 * H, H)), ((0, 2 * H), (2 * H, H)), ((0, 2 * H), (2 * H, H)), ((0, 2 * H), (2 * H, H)))
GATHER_PARTS = (((0, ZW // 2), (ZW // 2, ZW // 2)), ((0, ZW // 2), (ZW // 2, ZW // 2)), ((0, ZW // 2), (ZW // 2, ZW // 2)), ((0, ZW // 2), (ZW // 2, ZW // 2)), ((0, ZW // 2), (ZW // 2, ZW // 2)))
BY_LINE = (False,) * 4 + (True,)
PASSES = (4,) + (1,) * 4

A_A, A_B, A_D = 0, 3, 6
S_D, S_B, S_A = 10, 14, 17
R_R, R_L = 20, 28
G_R, G_L = 36, 44
Y_0 = 52
NSEM = 62


def enc4(v):
    t = v * jnp.abs(v) * (2.0**40)
    return (t * jnp.abs(t)).astype(BF)


def dec4(w):
    w = w.astype(F32)
    a = jnp.maximum(jnp.abs(w), 1e-37)
    r = lax.rsqrt(a)
    return (w * r) * (lax.rsqrt(a * r) * (2.0**-20))


def enc2(v):
    return (v * jnp.abs(v)).astype(BF)


def dec2(w):
    w = w.astype(F32)
    return w * lax.rsqrt(jnp.maximum(jnp.abs(w), 1e-37))


ORDER = (
    ("g0x", 0), ("g0y", 0), ("g0", 2), ("g0", 1), ("g1x", 0), ("g1y", 0), ("g1", 1), ("g1", 2),
    ("g2x", 0), ("g2y", 0), ("pj", 0, 0), ("r0", 0, 0), ("g2", 1), ("pj", 0, 1), ("r0", 0, 1),
    ("g0", 3), ("r1", 0, 0), ("r1", 0, 1), ("g2", 2), ("pj", 1, 0), ("r0", 1, 0), ("r2", 0, 0),
    ("pj", 1, 1), ("r0", 1, 1), ("g1", 3), ("r2", 0, 1), ("r1", 1, 0), ("pj", 2, 0),
    ("r0", 2, 0), ("g0", 4), ("r3", 0, 0), ("pj", 2, 1), ("r1", 1, 1), ("r3", 0, 1), ("g2", 3),
    ("r0", 2, 1), ("r1", 2, 0), ("r2", 1, 0), ("g1", 4), ("r2", 1, 1), ("ac", 0), ("r1", 2, 1),
    ("h0", 0, 0), ("pj", 3, 1), ("r0", 3, 1), ("r2", 2, 0), ("r3", 1, 0), ("r2", 2, 1),
    ("r3", 1, 1), ("pj", 3, 0), ("h1", 0, 0), ("h0", 0, 1), ("r3", 2, 0), ("r1", 3, 1),
    ("ac", 1), ("g2", 4), ("r0", 3, 0), ("r3", 2, 1), ("h2", 0, 0), ("h1", 0, 1), ("h0", 1, 1),
    ("h0", 1, 0), ("pj", 4, 1), ("h3", 0, 0), ("r1", 3, 0), ("pj", 4, 0), ("ac", 2),
    ("r0", 4, 0), ("r2", 3, 1), ("h4", 0, 0), ("h2", 0, 1), ("r0", 4, 1), ("h1", 1, 0),
    ("r2", 3, 0), ("h1", 1, 1), ("h3", 0, 1), ("r1", 4, 1), ("h0", 2, 1), ("h2", 1, 0),
    ("h0", 2, 0), ("h4", 0, 1), ("r3", 3, 0), ("h2", 1, 1), ("r1", 4, 0), ("r3", 3, 1),
    ("r2", 4, 1), ("wg", 0), ("h1", 2, 0), ("h3", 1, 1), ("tM", 0), ("h1", 2, 1), ("ac", 3),
    ("r2", 4, 0), ("h3", 1, 0), ("uM", 0), ("h2", 2, 0), ("h4", 1, 1), ("h2", 2, 1),
    ("r3", 4, 1), ("h0", 3, 1), ("h0", 3, 0), ("h4", 1, 0), ("tM", 1), ("r3", 4, 0), ("s2", 0),
    ("h3", 2, 1), ("wg", 1), ("h3", 2, 0), ("h1", 3, 1), ("h1", 3, 0), ("ac", 4), ("h4", 2, 1),
    ("h0", 4, 1), ("h0", 4, 0), ("h4", 2, 0), ("tM", 2), ("h2", 3, 1), ("uM", 1), ("h2", 3, 0),
    ("h1", 4, 1), ("uM", 2), ("h1", 4, 0), ("wg", 2), ("h3", 3, 1), ("h3", 3, 0), ("h2", 4, 1),
    ("s2", 1), ("h2", 4, 0), ("h4", 3, 1), ("h4", 3, 0), ("tM", 3), ("s2", 2), ("h3", 4, 1),
    ("h3", 4, 0), ("tA", 4), ("tB", 4), ("uM", 3), ("h4", 4, 1), ("uA", 4), ("h4", 4, 0),
    ("tC", 4), ("uB", 4), ("s3", 2), ("uC", 4), ("s3", 0), ("wg", 3), ("s2", 3), ("s2", 4),
    ("s3", 1), ("wg", 4), ("s3", 3), ("s3", 4),
)


def kernel(
    tok_hbm, cot_hbm, wg_hbm, wu_hbm, wd_hbm,
    gtok_hbm, gwg_hbm, gwu_hbm, gwd_hbm,
    xy, wgu, wd, part, rsend, rrecv, hid, gx, keep, dsend, drecv, bsend, brecv, asend, arecv,
    gtok, gwgu, gwd,
    ssem, rsem, lsem,
):
    r = lax.axis_index("row")
    c = lax.axis_index("col")
    core = lax.rem(c, 2)
    x = lax.rem(lax.div(c, 2), 4)
    y = lax.div(c, 8)
    a = x + core * (y - x)
    b = y + core * (x - y)

    def col(a_, b_):
        x_ = a_ + core * (b_ - a_)
        y_ = b_ + core * (a_ - b_)
        return y_ * 8 + x_ * 2 + core

    def m4(v):
        return lax.rem(v + 8, 4)

    def m8(v):
        return lax.rem(v + 16, 8)

    right = (m8(r + 1), c)
    left = (m8(r - 1), c)
    peer = (r, c + 1 - 2 * core)
    adev = {d: (r, col(m4(a + d), b)) for d in (1, 2, 3)}
    bdev = {d: (r, col(a, m4(b + d))) for d in (1, 2, 3)}
    place = core * 16 + b * 4 + a

    own_loads = [
        [
            pltpu.make_async_copy(
                src.at[pl.ds(s * RS, RS)], xy.at[s, place, k], lsem.at[2 * s + k]
            )
            for k, src in enumerate((tok_hbm, cot_hbm))
        ]
        for s in range(SLABS)
    ]
    weight_loads = [
        pltpu.make_async_copy(wg_hbm, wgu.at[:, pl.ds(0, H)], lsem.at[10]),
        pltpu.make_async_copy(wu_hbm, wgu.at[:, pl.ds(H, H)], lsem.at[11]),
        pltpu.make_async_copy(wd_hbm, wd, lsem.at[12]),
    ]
    for cp in sum(own_loads, []) + weight_loads:
        cp.start()

    barrier = pltpu.get_barrier_semaphore()
    partners = [right, left, peer] + [adev[d] for d in (1, 2, 3)] + [bdev[d] for d in (1, 2, 3)]
    for dev in partners:
        pl.semaphore_signal(barrier, inc=1, device_id=dev, device_id_type=MESH)
    pl.semaphore_wait(barrier, len(partners))

    sent = []

    def copy(src, dst, s, k, dev):
        return pltpu.make_async_remote_copy(
            src_ref=src, dst_ref=dst, send_sem=ssem.at[s, k], recv_sem=rsem.at[s, k],
            device_id=dev, device_id_type=MESH,
        )

    def send(src, dst, s, k, dev):
        cp = copy(src, dst, s, k, dev)
        cp.start()
        sent.append(cp)

    def recv(dst, s, k):
        copy(dst, dst, s, k, right).wait_recv()

    def pos(s, co, b_, a_, n=1, tag=""):
        at = pl.ds(co * 16 + b_ * 4 + a_, n)
        return xy.at[s, at, "xy".index(tag)] if tag else xy.at[s, at]

    def line(s, co, b_, tag=""):
        return pos(s, co, b_, 0, 4, tag)

    def chunk(ref, z, j, lo=0, n=CH):
        return ref.at[z, pl.ds(pl.multiple_of(j * CH + lo, 32), n)]

    def gather0(s, tag):
        k = Y_0 if tag == "y" else 0
        for cp in own_loads[s]["xy".index(tag) :][:1] if tag else own_loads[s]:
            cp.wait()
        me = pos(s, core, b, a, 1, tag)
        for d in (1, 2, 3):
            send(me, me, s, k + A_A + d - 1, adev[d])

    def gather1(s, tag):
        k = Y_0 if tag == "y" else 0
        for d in (1, 2, 3):
            recv(pos(s, core, b, m4(a - d), 1, tag), s, k + A_A + d - 1)
        row = line(s, core, b, tag)
        for d in (1, 2, 3):
            send(row, row, s, k + A_B + d - 1, bdev[d])
        if PASSES[s] == 4:
            send(row, row, s, k + A_D, peer)

    def half_of(s, co):
        return pos(s, co, 0, 0, 16)

    def gather2(s, tag):
        k = Y_0 if tag == "y" else 0
        for d in (1, 3, 2):
            row = line(s, core, m4(b - d), tag)
            recv(row, s, k + A_B + d - 1)
            if PASSES[s] == 4:
                send(row, row, s, k + A_D + d, peer)
        if PASSES[s] == 1:
            send(half_of(s, core), half_of(s, core), s, k + A_D, peer)

    ready = set()

    def project(s, f, both):
        first = s == 0 or s not in ready
        ready.add(s)
        for d in range(4) if PASSES[s] == 4 and first else ():
            tag, k = ("xy"[f], Y_0 * f) if s == 0 else ("", 0)
            recv(line(s, 1 - core, m4(a - d), tag), s, k + A_D + d)
        if PASSES[s] == 1 and first:
            recv(half_of(s, 1 - core), s, A_D)
        if s == 0:
            for cp in weight_loads[2 * f : 2 + f]:
                cp.wait()
        if f == 0:
            xs = xy[s, :, 0].reshape(32 * RS, W)
            part[s, :, 0 : 2 * H] = jnp.dot(xs, wgu[...], preferred_element_type=F32)
        if f == 1 or both:
            ys = xy[s, :, 1].reshape(32 * RS, W)
            part[s, :, 2 * H : ZW] = lax.dot_general(
                ys, wd[...], (((1,), (1,)), ((), ())), preferred_element_type=F32
            )

    def reduce_step(s, f, h):
        kr, kl = R_R + 4 * f, R_L + 4 * f
        lo, n = SUM_PARTS[s][f]
        lanes, cut = pl.ds(lo, n), slice(lo, lo + n)

        def mine(j, at=0, m=CH):
            return chunk(part, s, j, at, m)[:, cut]

        if h == 0:
            far = m8(r + 4)
            for way, dev, k in ((0, right, kr), (1, left, kl)):
                rsend[s, way, 0, 0:HALF, cut] = enc4(mine(far, HALF * way, HALF))
                send(
                    rsend.at[s, way, 0, pl.ds(0, HALF), lanes],
                    rrecv.at[s, way, 0, pl.ds(0, HALF), lanes],
                    s, k, dev,
                )
            return
        for way, dev, k, j in ((0, right, kr, m8(r + 4 - h)), (1, left, kl, m8(r - 4 + h))):
            if h == 1:
                recv(rrecv.at[s, way, 0, pl.ds(0, HALF), lanes], s, k)
                near, rest = (0, HALF) if way == 0 else (HALF, 0)
                rsend[s, way, 1, near : near + HALF, cut] = enc4(
                    mine(j, near, HALF) + dec4(rrecv[s, way, 0, 0:HALF, cut])
                )
                rsend[s, way, 1, rest : rest + HALF, cut] = enc4(mine(j, rest, HALF))
            else:
                recv(rrecv.at[s, way, h - 1, :, lanes], s, k + h - 1)
                rsend[s, way, h, :, cut] = enc4(mine(j) + dec4(rrecv[s, way, h - 1, :, cut]))
            send(rsend.at[s, way, h, :, lanes], rrecv.at[s, way, h, :, lanes], s, k + h, dev)

    def activate(s):
        for f, (lo, n) in enumerate(SUM_PARTS[s]):
            recv(rrecv.at[s, 0, 3, :, pl.ds(lo, n)], s, R_R + 4 * f + 3)
            recv(rrecv.at[s, 1, 3, :, pl.ds(lo, n)], s, R_L + 4 * f + 3)
        total = chunk(part, s, r)[...] + dec4(rrecv[s, 0, 3]) + dec4(rrecv[s, 1, 3])
        g, u, gh = total[:, 0:H], total[:, H : 2 * H], total[:, 2 * H :]
        sg = jax.nn.sigmoid(g)
        silu = g * sg
        out = chunk(hid, s, r)
        out[:, 0:H] = (gh * u * sg * (1.0 + g * (1.0 - sg))).astype(BF)
        out[:, H : 2 * H] = (gh * silu).astype(BF)
        out[:, 2 * H :] = (silu * u).astype(BF)

    def spread_step(s, f, h):
        lo_lane, n_lane = GATHER_PARTS[s][f]

        def part_of(j, at=0, m=CH):
            rows = pl.ds(pl.multiple_of(j * CH + at, 32), m)
            return hid.at[s, rows, pl.ds(lo_lane, n_lane)]

        kr, kl = G_R + 4 * f, G_L + 4 * f
        if h == 0:
            mine = part_of(r)
            send(mine, mine, s, kr, right)
            send(mine, mine, s, kl, left)
            return
        if h <= 3:
            lo, hi = part_of(m8(r - h)), part_of(m8(r + h))
            recv(lo, s, kr + h - 1)
            if h == 3:
                half = part_of(m8(r - 3), 0, HALF)
                send(half, half, s, kr + 3, right)
            else:
                send(lo, lo, s, kr + h, right)
            recv(hi, s, kl + h - 1)
            if h == 3:
                half = part_of(m8(r + 3), HALF, HALF)
                send(half, half, s, kl + 3, left)
            else:
                send(hi, hi, s, kl + h, left)
            return
        recv(part_of(m8(r + 4), 0, HALF), s, kr + 3)
        recv(part_of(m8(r + 4), HALF, HALF), s, kl + 3)

    order = [m4(r + 2), m4(r + 1), m4(r + 3), m4(r)]

    def token_grad(s, i):
        def rows_of(co):
            return lax.dot_general(
                chunk(hid, s, co * 4 + order[i])[:, 0 : 2 * H], wgu[...],
                (((1,), (1,)), ((), ())), preferred_element_type=F32,
            )

        dsend[s, i] = enc2(rows_of(1 - core))
        send(dsend.at[s, i], drecv.at[s, i], s, S_D + i, peer)
        gx[s % 2, i] = rows_of(core)

    def add_peer(s, i):
        recv(drecv.at[s, i], s, S_D + i)
        total = gx[s % 2, i] + dec2(drecv[s, i])
        d = m4(order[i] - b)

        @pl.when(d == 0)
        def _():
            keep[s % 2] = total

        @pl.when(d != 0)
        def _():
            bsend[s, i] = enc2(total)
            copy(
                bsend.at[s, i], brecv.at[s, d - 1], s, S_B + d - 1, (r, col(a, order[i]))
            ).start()

    def token_grad_whole(s):
        for co in (1 - core, core):
            rows = pl.ds(pl.multiple_of(co * 256, 256), 256)
            gx[s % 2] = lax.dot_general(
                hid[s, rows, 0 : 2 * H], wgu[...], (((1,), (1,)), ((), ())),
                preferred_element_type=F32,
            ).reshape(4, CH, W)
            if co is not core:
                dsend[s] = enc2(gx[s % 2])
                send(dsend.at[s], drecv.at[s], s, S_D, peer)

    def add_peer_whole(s):
        recv(drecv.at[s], s, S_D)
        gx[s % 2] = gx[s % 2] + dec2(drecv[s])
        for d in (1, 2, 3):
            bsend[s, d] = enc2(gx[s % 2, m4(b + d)])
            send(bsend.at[s, d], brecv.at[s, d - 1], s, S_B + d - 1, bdev[d])
        keep[s % 2] = gx[s % 2, b]

    def weight_grads(s):
        xs = xy[s, :, 0].reshape(32 * RS, W)
        ys = xy[s, :, 1].reshape(32 * RS, W)
        over = (((0,), (0,)), ((), ()))
        gu, hd = hid[s, :, 0 : 2 * H], hid[s, :, 2 * H :]
        dgu = lax.dot_general(xs, gu, over, preferred_element_type=F32)
        dd = lax.dot_general(hd, ys, over, preferred_element_type=F32)
        if s == 0:
            gwgu[...] = dgu
            gwd[...] = dd
        else:
            gwgu[...] += dgu
            gwd[...] += dd

    def scatter2(s):
        total = keep[s % 2]
        for d in (1, 2, 3):
            recv(brecv.at[s, d - 1], s, S_B + d - 1)
            total = total + dec2(brecv[s, d - 1])
        keep[s % 2] = total
        for d in (1, 2, 3):
            rows = pl.ds(pl.multiple_of(m4(a + d) * RS, RS), RS)
            asend[s, d - 1] = enc2(keep[s % 2, rows])
            send(asend.at[s, d - 1], arecv.at[s, d - 1], s, S_A + d - 1, adev[d])
        gtok[s * RS : (s + 1) * RS] = keep[s % 2, pl.ds(pl.multiple_of(a * RS, RS), RS)]

    def scatter3(s):
        total = gtok[s * RS : (s + 1) * RS]
        for d in (1, 2, 3):
            recv(arecv.at[s, d - 1], s, S_A + d - 1)
            total = total + dec2(arecv[s, d - 1])
        gtok[s * RS : (s + 1) * RS] = total

    def run(name, s, f=0):
        if name[0] == "r":
            reduce_step(s, f, int(name[1]))
        elif name[0] == "h":
            spread_step(s, f, int(name[1]))
        elif name in ("tM", "uM"):
            (token_grad_whole if name == "tM" else add_peer_whole)(s)
        elif name[0] == "t":
            for i in {"A": (0,), "B": (1, 2), "C": (3,)}[name[1]]:
                token_grad(s, i)
        elif name[0] == "u":
            for i in {"A": (0,), "B": (1, 2), "C": (3,)}[name[1]]:
                add_peer(s, i)
        elif name == "pj":
            project(s, f, len(SUM_PARTS[s]) == 1)
        elif name[0] == "g":
            (gather0, gather1, gather2)[int(name[1])](s, name[2:])
        else:
            {
                "ac": activate, "wg": weight_grads, "s2": scatter2, "s3": scatter3,
            }[name](s)

    for step in ORDER:
        run(*step)

    stores = [
        pltpu.make_async_copy(gtok, gtok_hbm, lsem.at[0]),
        pltpu.make_async_copy(gwd, gwd_hbm, lsem.at[1]),
    ]
    for k, dst in enumerate((gwg_hbm, gwu_hbm)):
        stores.append(
            pltpu.make_async_copy(gwgu.at[:, pl.ds(k * H, H)], dst, lsem.at[2 + k])
        )
    for cp in stores:
        cp.start()
    for cp in sent:
        cp.wait_send()
    for s in range(SLABS):
        for d in (1, 2, 3) if BY_LINE[s] else ():
            copy(bsend.at[s, 0], brecv.at[s, d - 1], s, S_B + d - 1, bdev[d]).wait_send()
    for cp in stores:
        cp.wait()


def write_out(*refs):
    ins, outs, bufs, sem_in, sem_out = refs[0:4], refs[4:8], refs[8:12], refs[12], refs[13]
    reads, writes = [], []
    for k, (src, buf, dst) in enumerate(zip(ins, bufs, outs)):
        n = src.shape[0] // 2
        for i in range(2):
            rows = pl.ds(i * n, n)
            reads.append(pltpu.make_async_copy(src.at[rows], buf.at[rows], sem_in.at[2 * k + i]))
            writes.append(pltpu.make_async_copy(buf.at[rows], dst.at[rows], sem_out.at[2 * k + i]))
    for cp in reads:
        cp.start()
    for rd, wr in zip(reads, writes):
        rd.wait()
        wr.start()
    for wr in writes:
        wr.wait()


def per_device(tokens, cotangent, gate_weight, up_weight, down_weight):
    hbm = pl.BlockSpec(memory_space=pl.ANY)
    rows = 32 * RS
    vm = pltpu.VMEM
    outs = pl.pallas_call(
        kernel,
        out_shape=(
            jax.ShapeDtypeStruct((SLABS * RS, W), F32),
            jax.ShapeDtypeStruct((W, H), F32),
            jax.ShapeDtypeStruct((W, H), F32),
            jax.ShapeDtypeStruct((H, W), F32),
        ),
        in_specs=[hbm] * 5,
        out_specs=[hbm] * 4,
        scratch_shapes=[
            vm((SLABS, 32, 2, RS, W), BF),
            vm((W, 2 * H), BF),
            vm((H, W), BF),
            vm((SLABS, rows, ZW), F32),
            vm((SLABS, 2, 4, CH, ZW), BF),
            vm((SLABS, 2, 4, CH, ZW), BF),
            vm((SLABS, rows, ZW), BF),
            vm((2, 4, CH, W), F32),
            vm((2, CH, W), F32),
            vm((SLABS, 4, CH, W), BF),
            vm((SLABS, 4, CH, W), BF),
            vm((SLABS, 4, CH, W), BF),
            vm((SLABS, 3, CH, W), BF),
            vm((SLABS, 3, RS, W), BF),
            vm((SLABS, 3, RS, W), BF),
            vm((SLABS * RS, W), F32),
            vm((W, 2 * H), F32),
            vm((H, W), F32),
            pltpu.SemaphoreType.DMA((SLABS, NSEM)),
            pltpu.SemaphoreType.DMA((SLABS, NSEM)),
            pltpu.SemaphoreType.DMA((15,)),
        ],
        compiler_params=pltpu.CompilerParams(
            collective_id=0, has_side_effects=True, vmem_limit_bytes=61 * 2**20
        ),
        name="swiglu_backward",
    )(tokens, cotangent, gate_weight, up_weight, down_weight)
    return pl.pallas_call(
        write_out,
        out_shape=[jax.ShapeDtypeStruct(o.shape, o.dtype) for o in outs],
        in_specs=[hbm] * 4,
        out_specs=[hbm] * 4,
        scratch_shapes=[vm(o.shape, o.dtype) for o in outs]
        + [pltpu.SemaphoreType.DMA((8,)), pltpu.SemaphoreType.DMA((8,))],
        name="write_out",
    )(*outs)


def solution(mesh):
    in_specs = (P("col", "row"), P("col", "row"), P("row", "col"), P("row", "col"), P("col", "row"))
    out_specs = (P("col", "row"), P("row", "col"), P("row", "col"), P("col", "row"))
    return jax.shard_map(
        per_device, mesh=mesh, in_specs=in_specs, out_specs=out_specs, check_vma=False
    )
```

time: 125 us -> 123 us (0.984)
    pallas_call x1, Pallas kernels: 122 us -> 120 us  [per_device(): pl.pallas_call(kernel, out_shape=(jax.ShapeDtypeStruct((SLABS * RS, W), F...]
where the time goes in v3:
time: 123 us
  Pallas kernels  123 us (100%)
    pallas_call x1, Pallas kernels, per_device(): pl.pallas_call(kernel, out_shape=(jax.ShapeDtypeStruct((SLABS * RS, W), F...  120 us
    pallas_call x1, Pallas kernels, per_device(): pl.pallas_call(write_out, out_shape=[jax.ShapeDtypeStruct(o.shape, o.dtyp...  2.48 us

profile of v3, /device:TPU:1, one launch (start us, length us, event | category | flops | bytes accessed | tf_op | source)
XLA Modules:
  0.0 123.4 jit_solution(16059630262474450673)
XLA Ops:
  0.6 120.1 %swiglu_backward.1 = (f32[80,640]{1,0:T(8,128)}, f32[640,256]{1,0:T(8,128)}, f32[640,256]{1,0:T(8,128)}, f32[256,640]{1,0:T(8,128)}) custom-call(bf16[80,640]{1,0:T(8,128)(2,1)} %tok_hbm.1, bf16[80,640]{1,0:T(8,128)(2,1)} %cot_hbm.1, bf16[640,256]{1,0:T(8,128)(2,1)} %wg_hbm.1, bf16[640,256]{1,0:T(8,128)(2,1)} %wu_hbm.1, bf16[256,640]{1,0:T(8,128)(2,1)} %wd_hbm.1), custom_call_target="tpu_custom_call" | custom-call | tf_op jit(solution)/shard_map/swiglu_backward/pallas_call | solution.py:439
  120.7 2.5 %write_out.1 = (f32[80,640]{1,0:T(8,128)}, f32[640,256]{1,0:T(8,128)}, f32[640,256]{1,0:T(8,128)}, f32[256,640]{1,0:T(8,128)}) custom-call(f32[80,640]{1,0:T(8,128)} %get-tuple-element.8.refs_0_, f32[640,256]{1,0:T(8,128)} %get-tuple-element.9.refs_1_, f32[640,256]{1,0:T(8,128)} %get-tuple-element.10.refs_2_, f32[256,640]{1,0:T(8,128)} %get-tuple-element.11.refs_3_), custom_call_target="tpu_custom_call" | custom-call | tf_op jit(solution)/shard_map/write_out/pallas_call | solution.py:477

commit v4 on v3

--- a/solution.py
+++ b/solution.py
@@ -392,25 +392,25 @@
                 "ac": activate, "wg": weight_grads, "s2": scatter2, "s3": scatter3,
             }[name](s)
 
+    weight_stores = [
+        pltpu.make_async_copy(gwd, gwd_hbm, lsem.at[1]),
+        pltpu.make_async_copy(gwgu.at[:, pl.ds(0, H)], gwg_hbm, lsem.at[2]),
+        pltpu.make_async_copy(gwgu.at[:, pl.ds(H, H)], gwu_hbm, lsem.at[3]),
+    ]
     for step in ORDER:
         run(*step)
-
-    stores = [
-        pltpu.make_async_copy(gtok, gtok_hbm, lsem.at[0]),
-        pltpu.make_async_copy(gwd, gwd_hbm, lsem.at[1]),
-    ]
-    for k, dst in enumerate((gwg_hbm, gwu_hbm)):
-        stores.append(
-            pltpu.make_async_copy(gwgu.at[:, pl.ds(k * H, H)], dst, lsem.at[2 + k])
-        )
-    for cp in stores:
-        cp.start()
+        if step == ("wg", SLABS - 1):
+            for cp in weight_stores:
+                cp.start()
+
+    token_store = pltpu.make_async_copy(gtok, gtok_hbm, lsem.at[0])
+    token_store.start()
     for cp in sent:
         cp.wait_send()
     for s in range(SLABS):
         for d in (1, 2, 3) if BY_LINE[s] else ():
             copy(bsend.at[s, 0], brecv.at[s, d - 1], s, S_B + d - 1, bdev[d]).wait_send()
-    for cp in stores:
+    for cp in weight_stores + [token_store]:
         cp.wait()
 
 

time: 123 us -> 123 us (level)
  no operation moved by 1% of the time
where the time goes in v4:
time: 123 us
  Pallas kernels  122 us (99%)
    pallas_call x1, Pallas kernels, per_device(): pl.pallas_call(kernel, out_shape=(jax.ShapeDtypeStruct((SLABS * RS, W), F...  119 us
    pallas_call x1, Pallas kernels, per_device(): pl.pallas_call(write_out, out_shape=[jax.ShapeDtypeStruct(o.shape, o.dtyp...  2.48 us

profile of v4, /device:TPU:1, one launch (start us, length us, event | category | flops | bytes accessed | tf_op | source)
XLA Modules:
  0.0 122.7 jit_solution(16653421833438109963)
XLA Ops:
  0.6 119.4 %swiglu_backward.1 = (f32[80,640]{1,0:T(8,128)}, f32[640,256]{1,0:T(8,128)}, f32[640,256]{1,0:T(8,128)}, f32[256,640]{1,0:T(8,128)}) custom-call(bf16[80,640]{1,0:T(8,128)(2,1)} %tok_hbm.1, bf16[80,640]{1,0:T(8,128)(2,1)} %cot_hbm.1, bf16[640,256]{1,0:T(8,128)(2,1)} %wg_hbm.1, bf16[640,256]{1,0:T(8,128)(2,1)} %wu_hbm.1, bf16[256,640]{1,0:T(8,128)(2,1)} %wd_hbm.1), custom_call_target="tpu_custom_call" | custom-call | tf_op jit(solution)/shard_map/swiglu_backward/pallas_call | solution.py:439
  120.0 2.5 %write_out.1 = (f32[80,640]{1,0:T(8,128)}, f32[640,256]{1,0:T(8,128)}, f32[640,256]{1,0:T(8,128)}, f32[256,640]{1,0:T(8,128)}) custom-call(f32[80,640]{1,0:T(8,128)} %get-tuple-element.8.refs_0_, f32[640,256]{1,0:T(8,128)} %get-tuple-element.9.refs_1_, f32[640,256]{1,0:T(8,128)} %get-tuple-element.10.refs_2_, f32[256,640]{1,0:T(8,128)} %get-tuple-element.11.refs_3_), custom_call_target="tpu_custom_call" | custom-call | tf_op jit(solution)/shard_map/write_out/pallas_call | solution.py:477
